TPU v7x, 128 devices: a whole 4x4x4 slice. The times are simulated.
128 devices in a mesh: spatial: 32 (over x, y, core), chan: 4 (over z).
Axes of the slice: x: 4, y: 4, z: 4, core: 2. Of those that a mesh axis runs over, the one named last changes fastest.
Arguments:
- fields: bfloat16 [1, 256, 737280], P(None, 'chan', 'spatial'), may hold values from -6 to 6
- mixing_weight: bfloat16 [2, 256, 256], P(None, 'chan'), may hold values from -0.25 to 0.25
- degree_gain: bfloat16 [640, 256], P(None, 'chan'), may hold values from 0.25 to 4
- cotangent: bfloat16 [1, 256, 737280], P(None, 'chan', 'spatial'), may hold values from -6 to 6
- order_ids: int32 [256], replicated, may hold values from 0 to 639, as said below
Outputs:
- output_field: bfloat16 [1, 256, 737280], P(None, 'chan', 'spatial')
- field_grad: bfloat16 [1, 256, 737280], P(None, 'chan', 'spatial')
- weight_grad: float32 [2, 256, 256], P(None, 'chan')
- gain_grad: float32 [640, 256], P(None, 'chan')
Inputs may be any that keep to these rules, and one draw needn't show every extreme that they name: `order_ids`: 256 distinct orders in ascending order; 0 and 639 are always among them.
All inputs are finite; a program needn't handle non-finite values.
Results may differ from a plain program's by a relative error of at most 0.022.
Values may be sent and summed in bfloat16 or wider, within the bound.
A program may use at most 128 MiB of HBM per device.

v0:
```python
import math

import jax
import jax.numpy as jnp
from jax import lax
from jax.experimental import pallas as pl
from jax.experimental.pallas import tpu as pltpu
from jax.sharding import PartitionSpec as P

MESH = pl.DeviceIdType.MESH
BF = jnp.bfloat16
F32 = jnp.float32

NLON = 1440
NLAT = 512
LMAX = 640
ORD = 256
NS = 32
NZ = 4
ND = NS * NZ
NXY = NS // 2
CD = 64
LD = 16
GROUP = 4 * NLON
WIN = 1536
STARTS = tuple((NLON * r) // 128 * 128 for r in range(4))
WROWS = 128
GROWS = 160
WCH = 16
GCH = 32
NG = 320 // GCH


def sincos(angle):
    h = angle * 0.5
    y = h * h
    s = y * (-1.0 / 39916800.0) + 1.0 / 362880.0
    s = s * y - 1.0 / 5040.0
    s = s * y + 1.0 / 120.0
    s = s * y - 1.0 / 6.0
    s = (s * y + 1.0) * h
    c = y * (1.0 / 479001600.0) - 1.0 / 3628800.0
    c = c * y + 1.0 / 40320.0
    c = c * y - 1.0 / 720.0
    c = c * y + 1.0 / 24.0
    c = c * y - 0.5
    c = c * y + 1.0
    return 2.0 * s * c, 1.0 - 2.0 * s * s


def turn(steps, period):
    rest = steps - period * jnp.floor(steps * (1.0 / period) + 0.5)
    return sincos(rest * (2.0 * math.pi / period))


def iota(shape, dim):
    return lax.broadcasted_iota(jnp.int32, shape, dim)


def gelu_parts(v):
    cdf = 0.5 * (1.0 + lax.erf(v * 0.7071067811865476))
    density = jnp.exp(-0.5 * v * v) * 0.3989422804014327
    return v * cdf, cdf + v * density


def low_half(shape):
    return iota(shape, 1) < 64


def swap_halves(a, b):
    low = low_half(a.shape)
    return (
        jnp.where(low, a, pltpu.roll(b, 64, 1)),
        jnp.where(low, pltpu.roll(a, 64, 1), b),
    )


def dot_nn(a, b):
    return lax.dot_general(a, b, (((1,), (0,)), ((), ())), preferred_element_type=F32)


def dot_nt(a, b):
    return lax.dot_general(a, b, (((1,), (1,)), ((), ())), preferred_element_type=F32)


def dot_tn(a, b):
    return lax.dot_general(a, b, (((0,), (0,)), ((), ())), preferred_element_type=F32)


def kernel(
    x_hbm, w_ref, gain_ref, cot_hbm, ords_ref, ords_smem,
    out_v, x_v, wgrad_ref, ggrad_ref,
    cot_v, tab, trig, leg, legt, scr,
    snd, rcv, gfold, wg, mat, gains,
    gsum, mixed, coeffs, spec, redw, redg, pairw, pairg, inw, ing, minew, mineg, finw, fing,
    in_sem, ssem, rsem, wsem, wrsem, dsem, drsem,
):
    s = lax.axis_index("spatial")
    z = lax.axis_index("chan")
    me = s * NZ + z
    core = s % 2
    xy = s // 2
    sibling = s + 1 - 2 * core
    barrier = pltpu.get_barrier_semaphore()

    def greet(i, carry):
        t = (me + i * 37) % ND
        pl.semaphore_signal(barrier, inc=1, device_id=(t // NZ, t % NZ), device_id_type=MESH)
        return carry

    lax.fori_loop(1, ND, greet, 0)
    x_in = pltpu.make_async_copy(x_hbm, x_v, in_sem.at[0])
    x_in.start()
    cot_in = pltpu.make_async_copy(cot_hbm, cot_v, in_sem.at[1])

    def fourier_table(i):
        row = jnp.broadcast_to(ords_ref[...].astype(F32), (ND, ORD))
        picked = iota((ND, ORD), 1) == 2 * iota((ND, ORD), 0) + i
        order_col = jnp.sum(jnp.where(picked, row, 0.0), axis=1, keepdims=True)
        lane = iota((ND, 384), 1)
        step = jnp.where(lane < 256, lane - 128, (lane - 256) * 128).astype(F32)
        sin_all, cos_all = turn(order_col * step, float(NLON))
        trig[0] = sin_all
        trig[1] = cos_all

        def some_rows(b, carry):
            rows = pl.ds(pl.multiple_of(b * 64, 64), 64)
            sin_row = trig[0, rows, :]
            cos_row = trig[1, rows, :]
            at = iota((64, 128), 1)
            shifted = []
            for r in range(4):
                lo = 128 - 32 * r
                shifted.append((sin_row[:, lo : lo + 128], cos_row[:, lo : lo + 128]))
            for q in range(12):
                sa = jnp.broadcast_to(sin_row[:, 256 + q : 257 + q], (64, 128))
                ca = jnp.broadcast_to(cos_row[:, 256 + q : 257 + q], (64, 128))
                for r in range(4):
                    sb, cb = shifted[r]
                    even = ca * cb - sa * sb
                    odd = -(sa * cb + ca * sb)
                    if q == 0 and r > 0:
                        even = jnp.where(at < 32 * r, 0.0, even)
                        odd = jnp.where(at < 32 * r, 0.0, odd)
                    if q == 11 and r < 3:
                        even = jnp.where(at >= 32 * r + 32, 0.0, even)
                        odd = jnp.where(at >= 32 * r + 32, 0.0, odd)
                    tab[r, i, 0, rows, q * 128 : q * 128 + 128] = even.astype(BF)
                    tab[r, i, 1, rows, q * 128 : q * 128 + 128] = odd.astype(BF)
            return carry

        lax.fori_loop(0, ND // 64, some_rows, 0)

    def start_all(phase, i, to_spectral, beside=None, count=0):
        k = phase * 2 + i

        def go(n, carry):
            t = (me + n * 37) % ND
            ts, tz = t // NZ, t % NZ
            if to_spectral:
                src, dst = snd.at[k, t], rcv.at[k, z * NS + s]
            else:
                src, dst = snd.at[k, tz * NS + ts], rcv.at[k, me]
            pltpu.make_async_remote_copy(
                src_ref=src, dst_ref=dst, send_sem=ssem.at[k], recv_sem=rsem.at[k],
                device_id=(ts, tz), device_id_type=MESH,
            ).start()
            return carry

        def go_both(n, carry):
            beside(n - 1)
            return go(n, carry)

        if count:
            lax.fori_loop(1, 1 + count, go_both, 0)
        lax.fori_loop(1 + count, ND, go, 0)
        if to_spectral:
            pltpu.make_async_copy(snd.at[k, me], rcv.at[k, z * NS + s], rsem.at[k]).start()
        else:
            pltpu.make_async_copy(snd.at[k, z * NS + s], rcv.at[k, me], rsem.at[k]).start()

    def wait_all(phase, i):
        k = phase * 2 + i
        pltpu.make_async_copy(rcv.at[k], rcv.at[k], rsem.at[k]).wait()

    def window(ref, r):
        return jnp.concatenate(
            [ref[:, g * GROUP + STARTS[r] : g * GROUP + STARTS[r] + WIN] for g in range(4)], axis=0
        )

    def table(r):
        return tab[r].reshape(2 * ORD, WIN)

    def fourier_tiles(data, r, factor, orders=(0, 1)):
        rows_of = tab[r].reshape(2 * ORD, WIN) if len(orders) == 2 else tab[r, orders[0]].reshape(ORD, WIN)
        prod = dot_nt(rows_of, data) * factor
        for n, i in enumerate(orders):
            rows = prod[n * ORD : n * ORD + ORD]
            for pair in range(2):
                lanes = slice(pair * 128, pair * 128 + 128)
                tiles = swap_halves(rows[:ND, lanes], rows[ND:, lanes])
                for m in range(2):
                    scr[i, pl.ds((pair * 2 + m) * 4 + r, ND, stride=LD), :] = tiles[m]

    def pack_send(phase, i):
        snd[phase * 2 + i] = scr[i].reshape(ND, LD, 128).astype(BF)

    def input_order(i):
        for r in range(4):
            fourier_tiles(window(x_v, r), r, 1.0 / math.sqrt(NLON), (i,))
        pack_send(0, i)

    fourier_table(0)
    x_in.wait()
    cot_in.start()
    input_order(0)
    pl.semaphore_wait(barrier, ND - 1)
    start_all(0, 0, True)
    fourier_table(1)
    input_order(1)

    gain_both = gain_ref[...].astype(F32)
    gain_both = jnp.transpose(jnp.concatenate([gain_both, gain_both], axis=0))
    folded = jnp.where(low_half((320, 128)), gain_both[:320], gain_both[320:])
    gfold[...] = folded.reshape(2, GROWS, 128).astype(BF)
    wg[z, core, 0:CD] = w_ref[core, :, 0:128]
    wg[z, core, CD:WROWS] = w_ref[core, :, 128:256]
    wg[z, core, WROWS : WROWS + GROWS] = gfold[core]

    def share_weights(n):
        dz = n % 3 + 1
        tile = wg.at[z, core, pl.ds(pl.multiple_of(n // 3 * 16, 16), 16)]
        pltpu.make_async_remote_copy(
            src_ref=tile, dst_ref=tile, send_sem=wsem.at[0], recv_sem=wrsem.at[dz],
            device_id=(s, (z + dz) % NZ), device_id_type=MESH,
        ).start()

    start_all(0, 1, True, share_weights, 3 * (WROWS + GROWS) // 16)

    order_here = [ords_smem[2 * me + i].astype(F32) for i in range(2)]
    phase_sc = []
    for i in range(2):
        phi = jnp.full((16, 128), 1.0, F32) * (order_here[i] * 0.37)
        turns = jnp.floor(phi * (1.0 / (2.0 * math.pi)) + 0.5)
        phi = (phi - turns * 6.28125) - turns * (2.0 * math.pi - 6.28125)
        phase_sc.append(sincos(phi))

    def with_phase(i, sn, cs):
        sp, cp = phase_sc[i]
        sp, cp = sp[:, :1], cp[:, :1]
        return sn * cp + cs * sp, cs * cp - sn * sp

    def legendre_rows(ref, width, blocks, degree_in_rows):
        odd = (2 * iota((16, width), 1) + 1).astype(F32)
        bs, bc = turn((2 * iota((16, width), 0) + 1).astype(F32) * odd, 4096.0)
        base = [with_phase(i, bs, bc) for i in range(2)]

        def rows(q, carry):
            first = q * 16
            sa, ca = turn((2 * first).astype(F32) * odd[:8], 4096.0)
            sa, ca = jnp.concatenate([sa, sa], axis=0), jnp.concatenate([ca, ca], axis=0)
            degree = first + iota((16, width), 0) if degree_in_rows else iota((16, width), 1)
            for i in range(2):
                sb, cb = base[i]
                value = jnp.where(degree.astype(F32) >= order_here[i], ca * cb - sa * sb, 0.0)
                ref[i, pl.ds(pl.multiple_of(first, 16), 16), :] = value.astype(BF)
            return carry

        lax.fori_loop(0, blocks, rows, 0)

    legendre_rows(leg, NLAT, LMAX // 16, True)
    legendre_rows(legt, LMAX, NLAT // 16, False)

    for dz in range(1, NZ):
        arrived = wg.at[(z + NZ - dz) % NZ, core]
        pltpu.make_async_copy(arrived, arrived, wrsem.at[dz]).wait()
    to_sibling = pltpu.make_async_remote_copy(
        src_ref=wg.at[:, core], dst_ref=wg.at[:, core], send_sem=wsem.at[1], recv_sem=wrsem.at[0],
        device_id=(sibling, z), device_id_type=MESH,
    )
    to_sibling.start()

    def project(phase, i):
        k = phase * 2 + i
        data = jnp.concatenate(
            [rcv[k, zz * NS : zz * NS + NS].reshape(NLAT, 128) for zz in range(NZ)], axis=1
        )
        return dot_nn(leg[i], data) * 0.0625

    def expand(phase, i):
        k = phase * 2 + i
        grid = dot_nn(legt[i], spec[i]) * 0.0625
        for zz in range(NZ):
            part = grid[:, zz * 128 : zz * 128 + 128].reshape(NS, LD, 128)
            snd[k, zz * NS : zz * NS + NS] = part.astype(BF)

    wait_all(0, 0)
    coeffs[0] = project(0, 0).astype(BF)

    to_sibling.wait_recv()
    for zz in range(NZ):
        for u in range(2):
            a = wg[zz, 0, u * CD : u * CD + CD].astype(F32)
            b = wg[zz, 1, u * CD : u * CD + CD].astype(F32)
            top = swap_halves(a, b)
            low = swap_halves(-b, a)
            for n in range(2):
                lanes = slice((2 * u + n) * 128, (2 * u + n) * 128 + 128)
                mat[zz * 128 : zz * 128 + CD, lanes] = top[n].astype(BF)
                mat[zz * 128 + CD : zz * 128 + 128, lanes] = low[n].astype(BF)
        fold = wg[zz, :, WROWS : WROWS + GROWS].astype(F32).reshape(320, 128)
        both = pltpu.roll(fold, 64, 1)
        low = low_half((320, 128))
        gains[0:320, zz * 128 : zz * 128 + 128] = jnp.where(low, fold, both).astype(BF)
        gains[320:640, zz * 128 : zz * 128 + 128] = jnp.where(low, both, fold).astype(BF)

    def mix(i):
        prod = dot_nn(coeffs[i], mat[...])
        mixed[i] = prod
        spec[i] = (gains[...].astype(F32) * prod).astype(BF)
        expand(1, i)
        start_all(1, i, False)

    mix(0)
    wait_all(0, 1)
    coeffs[1] = project(0, 1).astype(BF)
    mix(1)

    def order_rows(r):
        parts = []
        for i in range(2):
            tiles = [scr[i, pl.ds(4 * g + r, ND, stride=LD), :] for g in range(4)]
            pairs = [swap_halves(tiles[0], tiles[1]), swap_halves(tiles[2], tiles[3])]
            parts += [jnp.concatenate([pairs[0][p], pairs[1][p]], axis=1) for p in range(2)]
        return jnp.concatenate(parts, axis=0).astype(BF)

    def unpack(phase, i):
        wait_all(phase, i)
        scr[i] = rcv[phase * 2 + i].astype(F32).reshape(ND * LD, 128)

    def put_window(ref, r, value):
        for g in range(4):
            part = value[g * CD : g * CD + CD]
            lo = g * GROUP + STARTS[r]
            if r > 0:
                first = ref[:, lo : lo + 128].astype(F32) + part[:, :128]
                ref[:, lo : lo + 128] = first.astype(BF)
                ref[:, lo + 128 : lo + WIN] = part[:, 128:].astype(BF)
            else:
                ref[:, lo : lo + WIN] = part.astype(BF)

    cot_in.wait()
    unpack(1, 0)
    unpack(1, 1)
    rows = [order_rows(r) for r in range(4)]
    for r in range(4):
        before = dot_tn(rows[r], table(r)) * 0.0625
        value, slope = gelu_parts(before)
        put_window(out_v, r, value)
        grad = (window(cot_v, r).astype(F32) * slope).astype(BF)
        fourier_tiles(grad, r, 0.0625)
    for i in range(2):
        pack_send(2, i)
        start_all(2, i, True)

    def back(i):
        wait_all(2, i)
        value = project(2, i)
        here = value * mixed[i]
        gsum[...] = here if i == 0 else gsum[...] + here
        spec[i] = (gains[...].astype(F32) * value).astype(BF)
        if i == 0:
            wpart = dot_tn(coeffs[0], spec[0])
            mixed[0, :512] = wpart
        else:
            wpart = dot_tn(coeffs[1], spec[1]) + mixed[0, :512]
            sign = jnp.where(low_half((CD, 128)), 1.0, -1.0)
            for zz in range(NZ):
                for zo in range(NZ):
                    lanes = slice(zo * 128, zo * 128 + 128)
                    up = wpart[zz * 128 : zz * 128 + CD, lanes]
                    down = wpart[zz * 128 + CD : zz * 128 + 128, lanes]
                    redw[zz, zo * CD : zo * CD + CD] = (up + pltpu.roll(down, 64, 1) * sign).astype(BF)
                both = gsum[:, zz * 128 : zz * 128 + 128]
                both = both + pltpu.roll(both, 64, 1)
                redg[zz] = jnp.where(low_half((320, 128)), both[:320], both[320:]).astype(BF)

    def to_inputs(i):
        spec[i] = dot_nt(spec[i], mat[...]).astype(BF)

    back(0)
    to_inputs(0)
    expand(3, 0)
    start_all(3, 0, False)
    back(1)

    @pl.when(core == 0)
    def _():
        pltpu.make_async_remote_copy(
            src_ref=redg, dst_ref=pairg, send_sem=dsem.at[0], recv_sem=drsem.at[0],
            device_id=(sibling, z), device_id_type=MESH,
        ).start()

    @pl.when(core == 1)
    def _():
        pltpu.make_async_remote_copy(
            src_ref=redw, dst_ref=pairw, send_sem=dsem.at[0], recv_sem=drsem.at[0],
            device_id=(sibling, z), device_id_type=MESH,
        ).start()

    to_inputs(1)
    expand(3, 1)

    source = xy * NZ + z

    @pl.when(core == 0)
    def _():
        pltpu.make_async_copy(pairw, pairw, drsem.at[0]).wait()
        pairw[...] = (pairw[...].astype(F32) + redw[...].astype(F32)).astype(BF)

        def go(n, carry):
            t = (source + n * 37) % (NXY * NZ)
            txy, tz = t // NZ, t % NZ
            pltpu.make_async_remote_copy(
                src_ref=pairw.at[tz, pl.ds(pl.multiple_of(txy * WCH, WCH), WCH)], dst_ref=inw.at[source],
                send_sem=dsem.at[1], recv_sem=drsem.at[1], device_id=(txy * 2, tz), device_id_type=MESH,
            ).start()
            return carry

        lax.fori_loop(1, NXY * NZ, go, 0)
        pltpu.make_async_copy(
            pairw.at[z, pl.ds(pl.multiple_of(xy * WCH, WCH), WCH)], inw.at[source], drsem.at[1]
        ).start()

    chunk = (xy * 5 + 7) // 8
    adds_gain = (chunk * 8) // 5 == xy

    @pl.when(core == 1)
    def _():
        pltpu.make_async_copy(pairg, pairg, drsem.at[0]).wait()
        pairg[...] = (pairg[...].astype(F32) + redg[...].astype(F32)).astype(BF)

        def go(n, carry):
            ch, tz = n % NG, (z + n // NG) % NZ
            txy = (ch * 8) // 5

            @pl.when(txy * NZ + tz != source)
            def _():
                pltpu.make_async_remote_copy(
                    src_ref=pairg.at[tz, pl.ds(pl.multiple_of(ch * GCH, GCH), GCH)], dst_ref=ing.at[source],
                    send_sem=dsem.at[2], recv_sem=drsem.at[2], device_id=(txy * 2 + 1, tz), device_id_type=MESH,
                ).start()

            @pl.when(txy * NZ + tz == source)
            def _():
                pltpu.make_async_copy(
                    pairg.at[tz, pl.ds(pl.multiple_of(ch * GCH, GCH), GCH)], ing.at[source], drsem.at[2]
                ).start()

            return carry

        lax.fori_loop(0, NG * NZ, go, 0)

    start_all(3, 1, False)

    def share(mine, fin, at, sem):
        def go(n, carry):
            pltpu.make_async_remote_copy(
                src_ref=mine, dst_ref=fin.at[at], send_sem=dsem.at[sem], recv_sem=drsem.at[sem],
                device_id=((s + n) % NS, z), device_id_type=MESH,
            ).start()
            return carry

        lax.fori_loop(1, NS, go, 0)
        pltpu.make_async_copy(mine, fin.at[at], drsem.at[sem]).start()

    unpack(3, 0)

    @pl.when(core == 0)
    def _():
        pltpu.make_async_copy(inw, inw, drsem.at[1]).wait()
        minew[...] = jnp.sum(inw[...].astype(F32), axis=0).astype(BF)
        share(minew, finw, xy, 3)

    @pl.when(jnp.logical_and(core == 1, adds_gain))
    def _():
        pltpu.make_async_copy(ing, ing, drsem.at[2]).wait()
        mineg[...] = jnp.sum(ing[...].astype(F32), axis=0).astype(BF)
        share(mineg, fing, chunk, 4)

    unpack(3, 1)
    rows = [order_rows(r) for r in range(4)]
    for r in range(4):
        put_window(x_v, r, dot_tn(rows[r], table(r)) * (1.0 / math.sqrt(NLON)))

    pltpu.make_async_copy(finw, finw, drsem.at[3]).wait()
    pltpu.make_async_copy(fing, fing, drsem.at[4]).wait()
    wscale = 1.0 / math.sqrt(ORD * LMAX)
    sums = finw[...].astype(F32).reshape(NZ, CD, 128) * wscale
    for u in range(2):
        pair = swap_halves(sums[2 * u], sums[2 * u + 1])
        for p in range(2):
            wgrad_ref[p, :, u * 128 : u * 128 + 128] = pair[p]
    fold = fing[...].astype(F32).reshape(320, 128) * (1.0 / math.sqrt(ORD))
    ggrad_ref[...] = jnp.transpose(jnp.concatenate([fold, pltpu.roll(fold, 64, 1)], axis=0))[:CD]

    for k in range(8):
        pltpu.make_async_copy(snd.at[k, pl.ds(0, ND - 1)], snd.at[k, pl.ds(0, ND - 1)], ssem.at[k]).wait()
    for dz in range(1, NZ):
        pltpu.make_async_copy(wg.at[z, core], wg.at[z, core], wsem.at[0]).wait()
    to_sibling.wait_send()

    @pl.when(core == 0)
    def _():
        pltpu.make_async_copy(redg, redg, dsem.at[0]).wait()
        others = NXY * NZ - 1
        pltpu.make_async_copy(inw.at[pl.ds(0, others)], inw.at[pl.ds(0, others)], dsem.at[1]).wait()
        pltpu.make_async_copy(sent(finw), sent(finw), dsem.at[3]).wait()
        pltpu.make_async_copy(rest(finw), rest(finw), dsem.at[3]).wait()

    @pl.when(core == 1)
    def _():
        pltpu.make_async_copy(redw, redw, dsem.at[0]).wait()

        @pl.when(adds_gain)
        def _():
            others = NG * NZ - 1
            pltpu.make_async_copy(ing.at[pl.ds(0, others)], ing.at[pl.ds(0, others)], dsem.at[2]).wait()
            for _ in range(3):
                pltpu.make_async_copy(fing, fing, dsem.at[4]).wait()
            pltpu.make_async_copy(mineg, mineg, dsem.at[4]).wait()

        @pl.when(jnp.logical_not(adds_gain))
        def _():
            others = NG * NZ
            pltpu.make_async_copy(ing.at[pl.ds(0, others)], ing.at[pl.ds(0, others)], dsem.at[2]).wait()


def sent(fin):
    return fin.at[pl.ds(0, NXY)]


def rest(fin):
    return fin.at[pl.ds(0, NXY - 1)]


def finish(*refs):
    sem = refs[-1]
    copies = [pltpu.make_async_copy(refs[i], refs[4 + i], sem.at[i]) for i in range(4)]
    for copy in copies:
        copy.start()
    for copy in copies:
        copy.wait()


def body(fields, mixing_weight, degree_gain, cotangent, order_ids):
    cells = fields.shape[2]
    vmem = pl.BlockSpec(memory_space=pltpu.VMEM)
    anyw = pl.BlockSpec(memory_space=pl.ANY)
    smem = pl.BlockSpec(memory_space=pltpu.SMEM)
    shapes = (
        ((CD, cells), BF),
        ((CD, cells), BF),
        ((2, CD, 256), F32),
        ((CD, LMAX), F32),
    )
    results = pl.pallas_call(
        kernel,
        out_shape=tuple(pltpu.VMEM(shape, kind) for shape, kind in shapes),
        in_specs=[anyw, vmem, vmem, anyw, vmem, smem],
        out_specs=(vmem,) * 4,
        scratch_shapes=[
            pltpu.VMEM((CD, cells), BF),
            pltpu.VMEM((4, 2, 2, ND, WIN), BF),
            pltpu.VMEM((2, ND, 384), F32),
            pltpu.VMEM((2, LMAX, NLAT), BF),
            pltpu.VMEM((2, NLAT, LMAX), BF),
            pltpu.VMEM((2, ND * LD, 128), F32),
            pltpu.VMEM((8, ND, LD, 128), BF),
            pltpu.VMEM((8, ND, LD, 128), BF),
            pltpu.VMEM((2, GROWS, 128), BF),
            pltpu.VMEM((NZ, 2, WROWS + GROWS, 128), BF),
            pltpu.VMEM((512, 512), BF),
            pltpu.VMEM((LMAX, 512), BF),
            pltpu.VMEM((LMAX, 512), F32),
            pltpu.VMEM((2, LMAX, 512), F32),
            pltpu.VMEM((2, LMAX, 512), BF),
            pltpu.VMEM((2, LMAX, 512), BF),
            pltpu.VMEM((NZ, 256, 128), BF),
            pltpu.VMEM((NZ, 320, 128), BF),
            pltpu.VMEM((NZ, 256, 128), BF),
            pltpu.VMEM((NZ, 320, 128), BF),
            pltpu.VMEM((NXY * NZ, WCH, 128), BF),
            pltpu.VMEM((NXY * NZ, GCH, 128), BF),
            pltpu.VMEM((WCH, 128), BF),
            pltpu.VMEM((GCH, 128), BF),
            pltpu.VMEM((NXY, WCH, 128), BF),
            pltpu.VMEM((NG, GCH, 128), BF),
            pltpu.SemaphoreType.DMA((2,)),
            pltpu.SemaphoreType.DMA((8,)),
            pltpu.SemaphoreType.DMA((8,)),
            pltpu.SemaphoreType.DMA((2,)),
            pltpu.SemaphoreType.DMA((4,)),
            pltpu.SemaphoreType.DMA((5,)),
            pltpu.SemaphoreType.DMA((5,)),
        ],
        compiler_params=pltpu.CompilerParams(
            collective_id=0, has_side_effects=True, vmem_limit_bytes=50 << 20
        ),
    )(
        fields.reshape(CD, cells), mixing_weight, degree_gain.T, cotangent.reshape(CD, cells),
        order_ids.reshape(1, ORD), order_ids,
    )
    out, fgrad, wgrad, ggrad = pl.pallas_call(
        finish,
        out_shape=tuple(jax.ShapeDtypeStruct(shape, kind) for shape, kind in shapes),
        in_specs=[anyw] * 4,
        out_specs=(anyw,) * 4,
        scratch_shapes=[pltpu.SemaphoreType.DMA((4,))],
        compiler_params=pltpu.CompilerParams(vmem_limit_bytes=1 << 20),
    )(*[pltpu.with_memory_space_constraint(a, pltpu.VMEM) for a in results])
    return out.reshape(1, CD, cells), fgrad.reshape(1, CD, cells), wgrad, ggrad.T


def solution(mesh):
    return jax.shard_map(
        body,
        mesh=mesh,
        in_specs=(
            P(None, "chan", "spatial"),
            P(None, "chan", None),
            P(None, "chan"),
            P(None, "chan", "spatial"),
            P(),
        ),
        out_specs=(
            P(None, "chan", "spatial"),
            P(None, "chan", "spatial"),
            P(None, "chan", None),
            P(None, "chan"),
        ),
        check_vma=False,
    )
```

profile of v0, /device:TPU:1, one launch (start us, length us, event | category | flops | bytes accessed | tf_op | source)
XLA Modules:
  0.0 98.3 jit_solution(3720189500028010907)
XLA Ops:
  0.6 94.8 %shard_map.84 = (bf16[64,23040]{1,0:T(8,128)(2,1)S(1)}, bf16[64,23040]{1,0:T(8,128)(2,1)S(1)}, f32[2,64,256]{2,1,0:T(8,128)S(1)}, f32[64,640]{1,0:T(8,128)S(1)}) custom-call(bf16[64,23040]{1,0:T(8,128)(2,1)} %bitcast.7, bf16[2,64,256]{2,1,0:T(8,128)(2,1)} %w_ref.1, bf16[64,640]{1,0:T(8,128)(2,1)} %bitcast.9, bf16[64,23040]{1,0:T(8,128)(2,1)} %bitcast.8, ...), custom_call_target="tpu_custom_call" | custom-call | tf_op jit(solution)/shard_map/pallas_call | solution.py:567
  95.4 2.7 %shard_map.85 = (bf16[64,23040]{1,0:T(8,128)(2,1)}, bf16[64,23040]{1,0:T(8,128)(2,1)}, f32[2,64,256]{2,1,0:T(8,128)}, f32[64,640]{1,0:T(8,128)}) custom-call(bf16[64,23040]{1,0:T(8,128)(2,1)S(1)} %get-tuple-element.12.refs_0_, bf16[64,23040]{1,0:T(8,128)(2,1)S(1)} %get-tuple-element.13.refs_1_, f32[2,64,256]{2,1,0:T(8,128)S(1)} %get-tuple-element.14.refs_2_, ...), custom_call_target="tpu_custom_call" | custom-call | tf_op jit(solution)/shard_map/pallas_call | solution.py:614
where the time goes:
time: 98.4 us; the launch traced here: 98.3 us
  Pallas kernels  97.5 us (99%)
    pallas_call x1, Pallas kernels, body(): pl.pallas_call(kernel, out_shape=tuple((pltpu.VMEM(shape, kind) for shape...  94.8 us
    pallas_call x1, Pallas kernels, body(): pl.pallas_call(finish, out_shape=tuple((jax.ShapeDtypeStruct(shape, kind)...  2.68 us

commit v1 on v0

--- a/solution.py
+++ b/solution.py
@@ -90,7 +90,7 @@
 def kernel(
     x_hbm, w_ref, gain_ref, cot_hbm, ords_ref, ords_smem,
     out_v, x_v, wgrad_ref, ggrad_ref,
-    cot_v, tab, trig, leg, legt, scr,
+    cot_v, tab, trig, leg, legt, scr, partial, grads,
     snd, rcv, gfold, wg, mat, gains,
     gsum, mixed, coeffs, spec, redw, redg, pairw, pairg, inw, ing, minew, mineg, finw, fing,
     in_sem, ssem, rsem, wsem, wrsem, dsem, drsem,
@@ -188,36 +188,21 @@
             [ref[:, g * GROUP + STARTS[r] : g * GROUP + STARTS[r] + WIN] for g in range(4)], axis=0
         )
 
-    def table(r):
-        return tab[r].reshape(2 * ORD, WIN)
-
-    def fourier_tiles(data, r, factor, orders=(0, 1)):
-        rows_of = tab[r].reshape(2 * ORD, WIN) if len(orders) == 2 else tab[r, orders[0]].reshape(ORD, WIN)
-        prod = dot_nt(rows_of, data) * factor
-        for n, i in enumerate(orders):
-            rows = prod[n * ORD : n * ORD + ORD]
-            for pair in range(2):
-                lanes = slice(pair * 128, pair * 128 + 128)
-                tiles = swap_halves(rows[:ND, lanes], rows[ND:, lanes])
-                for m in range(2):
-                    scr[i, pl.ds((pair * 2 + m) * 4 + r, ND, stride=LD), :] = tiles[m]
+    def fourier_tiles(i, data, r, factor):
+        prod = dot_nt(tab[r, i].reshape(ORD, WIN), data) * factor
+        for pair in range(2):
+            lanes = slice(pair * 128, pair * 128 + 128)
+            tiles = swap_halves(prod[:ND, lanes], prod[ND:, lanes])
+            for m in range(2):
+                scr[i, pl.ds((pair * 2 + m) * 4 + r, ND, stride=LD), :] = tiles[m]
 
     def pack_send(phase, i):
         snd[phase * 2 + i] = scr[i].reshape(ND, LD, 128).astype(BF)
 
     def input_order(i):
         for r in range(4):
-            fourier_tiles(window(x_v, r), r, 1.0 / math.sqrt(NLON), (i,))
+            fourier_tiles(i, window(x_v, r), r, 1.0 / math.sqrt(NLON))
         pack_send(0, i)
-
-    fourier_table(0)
-    x_in.wait()
-    cot_in.start()
-    input_order(0)
-    pl.semaphore_wait(barrier, ND - 1)
-    start_all(0, 0, True)
-    fourier_table(1)
-    input_order(1)
 
     gain_both = gain_ref[...].astype(F32)
     gain_both = jnp.transpose(jnp.concatenate([gain_both, gain_both], axis=0))
@@ -235,7 +220,16 @@
             device_id=(s, (z + dz) % NZ), device_id_type=MESH,
         ).start()
 
-    start_all(0, 1, True, share_weights, 3 * (WROWS + GROWS) // 16)
+    fourier_table(0)
+    x_in.wait()
+    cot_in.start()
+    input_order(0)
+    pl.semaphore_wait(barrier, ND - 1)
+    start_all(0, 0, True, share_weights, 3 * (WROWS + GROWS) // 16)
+    fourier_table(1)
+    input_order(1)
+
+    start_all(0, 1, True)
 
     order_here = [ords_smem[2 * me + i].astype(F32) for i in range(2)]
     phase_sc = []
@@ -326,17 +320,23 @@
     coeffs[1] = project(0, 1).astype(BF)
     mix(1)
 
-    def order_rows(r):
-        parts = []
-        for i in range(2):
-            tiles = [scr[i, pl.ds(4 * g + r, ND, stride=LD), :] for g in range(4)]
-            pairs = [swap_halves(tiles[0], tiles[1]), swap_halves(tiles[2], tiles[3])]
-            parts += [jnp.concatenate([pairs[0][p], pairs[1][p]], axis=1) for p in range(2)]
+    def order_rows(i, r):
+        tiles = [scr[i, pl.ds(4 * g + r, ND, stride=LD), :] for g in range(4)]
+        pairs = [swap_halves(tiles[0], tiles[1]), swap_halves(tiles[2], tiles[3])]
+        parts = [jnp.concatenate([pairs[0][p], pairs[1][p]], axis=1) for p in range(2)]
         return jnp.concatenate(parts, axis=0).astype(BF)
 
     def unpack(phase, i):
         wait_all(phase, i)
         scr[i] = rcv[phase * 2 + i].astype(F32).reshape(ND * LD, 128)
+
+    def grid_part(i, r):
+        return dot_tn(order_rows(i, r), tab[r, i].reshape(ORD, WIN))
+
+    def first_part(phase):
+        unpack(phase, 0)
+        for r in range(4):
+            partial[r] = grid_part(0, r)
 
     def put_window(ref, r, value):
         for g in range(4):
@@ -350,18 +350,20 @@
                 ref[:, lo : lo + WIN] = part.astype(BF)
 
     cot_in.wait()
-    unpack(1, 0)
+    first_part(1)
     unpack(1, 1)
-    rows = [order_rows(r) for r in range(4)]
     for r in range(4):
-        before = dot_tn(rows[r], table(r)) * 0.0625
+        before = (partial[r] + grid_part(1, r)) * 0.0625
         value, slope = gelu_parts(before)
         put_window(out_v, r, value)
-        grad = (window(cot_v, r).astype(F32) * slope).astype(BF)
-        fourier_tiles(grad, r, 0.0625)
-    for i in range(2):
-        pack_send(2, i)
-        start_all(2, i, True)
+        grads[r] = (window(cot_v, r).astype(F32) * slope).astype(BF)
+        fourier_tiles(0, grads[r], r, 0.0625)
+    pack_send(2, 0)
+    start_all(2, 0, True)
+    for r in range(4):
+        fourier_tiles(1, grads[r], r, 0.0625)
+    pack_send(2, 1)
+    start_all(2, 1, True)
 
     def back(i):
         wait_all(2, i)
@@ -474,7 +476,7 @@
         lax.fori_loop(1, NS, go, 0)
         pltpu.make_async_copy(mine, fin.at[at], drsem.at[sem]).start()
 
-    unpack(3, 0)
+    first_part(3)
 
     @pl.when(core == 0)
     def _():
@@ -489,9 +491,8 @@
         share(mineg, fing, chunk, 4)
 
     unpack(3, 1)
-    rows = [order_rows(r) for r in range(4)]
     for r in range(4):
-        put_window(x_v, r, dot_tn(rows[r], table(r)) * (1.0 / math.sqrt(NLON)))
+        put_window(x_v, r, (partial[r] + grid_part(1, r)) * (1.0 / math.sqrt(NLON)))
 
     pltpu.make_async_copy(finw, finw, drsem.at[3]).wait()
     pltpu.make_async_copy(fing, fing, drsem.at[4]).wait()
@@ -576,6 +577,8 @@
             pltpu.VMEM((2, LMAX, NLAT), BF),
             pltpu.VMEM((2, NLAT, LMAX), BF),
             pltpu.VMEM((2, ND * LD, 128), F32),
+            pltpu.VMEM((4, 256, WIN), F32),
+            pltpu.VMEM((4, 256, WIN), BF),
             pltpu.VMEM((8, ND, LD, 128), BF),
             pltpu.VMEM((8, ND, LD, 128), BF),
             pltpu.VMEM((2, GROWS, 128), BF),

time: 98.4 us -> 93.2 us (0.947)
  Pallas kernels: 97.5 us -> 92.3 us
    pallas_call x1, Pallas kernels: 94.8 us -> 89.6 us  [body(): pl.pallas_call(kernel, out_shape=tuple((pltpu.VMEM(shape, kind) for shape...]
where the time goes in v1:
time: 93.2 us; the launch traced here: 93.1 us
  Pallas kernels  92.3 us (99%)
    pallas_call x1, Pallas kernels, body(): pl.pallas_call(kernel, out_shape=tuple((pltpu.VMEM(shape, kind) for shape...  89.6 us
    pallas_call x1, Pallas kernels, body(): pl.pallas_call(finish, out_shape=tuple((jax.ShapeDtypeStruct(shape, kind)...  2.68 us

profile of v1, /device:TPU:1, one launch (start us, length us, event | category | flops | bytes accessed | tf_op | source)
XLA Modules:
  0.0 93.1 jit_solution(14732168303411468257)
XLA Ops:
  0.6 89.6 %shard_map.84 = (bf16[64,23040]{1,0:T(8,128)(2,1)S(1)}, bf16[64,23040]{1,0:T(8,128)(2,1)S(1)}, f32[2,64,256]{2,1,0:T(8,128)S(1)}, f32[64,640]{1,0:T(8,128)S(1)}) custom-call(bf16[64,23040]{1,0:T(8,128)(2,1)} %bitcast.7, bf16[2,64,256]{2,1,0:T(8,128)(2,1)} %w_ref.1, bf16[64,640]{1,0:T(8,128)(2,1)} %bitcast.9, bf16[64,23040]{1,0:T(8,128)(2,1)} %bitcast.8, ...), custom_call_target="tpu_custom_call" | custom-call | tf_op jit(solution)/shard_map/pallas_call | solution.py:568
  90.2 2.7 %shard_map.85 = (bf16[64,23040]{1,0:T(8,128)(2,1)}, bf16[64,23040]{1,0:T(8,128)(2,1)}, f32[2,64,256]{2,1,0:T(8,128)}, f32[64,640]{1,0:T(8,128)}) custom-call(bf16[64,23040]{1,0:T(8,128)(2,1)S(1)} %get-tuple-element.12.refs_0_, bf16[64,23040]{1,0:T(8,128)(2,1)S(1)} %get-tuple-element.13.refs_1_, f32[2,64,256]{2,1,0:T(8,128)S(1)} %get-tuple-element.14.refs_2_, ...), custom_call_target="tpu_custom_call" | custom-call | tf_op jit(solution)/shard_map/pallas_call | solution.py:617

commit v2 on v1

--- a/solution.py
+++ b/solution.py
@@ -103,14 +103,15 @@
     sibling = s + 1 - 2 * core
     barrier = pltpu.get_barrier_semaphore()
 
+    x_in = pltpu.make_async_copy(x_hbm, x_v, in_sem.at[0])
+    x_in.start()
+
     def greet(i, carry):
         t = (me + i * 37) % ND
         pl.semaphore_signal(barrier, inc=1, device_id=(t // NZ, t % NZ), device_id_type=MESH)
         return carry
 
     lax.fori_loop(1, ND, greet, 0)
-    x_in = pltpu.make_async_copy(x_hbm, x_v, in_sem.at[0])
-    x_in.start()
     cot_in = pltpu.make_async_copy(cot_hbm, cot_v, in_sem.at[1])
 
     def fourier_table(i):
@@ -412,6 +413,7 @@
 
     to_inputs(1)
     expand(3, 1)
+    start_all(3, 1, False)
 
     source = xy * NZ + z
 
@@ -462,8 +464,6 @@
             return carry
 
         lax.fori_loop(0, NG * NZ, go, 0)
-
-    start_all(3, 1, False)
 
     def share(mine, fin, at, sem):
         def go(n, carry):
@@ -547,7 +547,13 @@
 
 def finish(*refs):
     sem = refs[-1]
-    copies = [pltpu.make_async_copy(refs[i], refs[4 + i], sem.at[i]) for i in range(4)]
+    copies = [pltpu.make_async_copy(refs[i], refs[4 + i], sem.at[i]) for i in range(2, 4)]
+    for n in range(4):
+        rows = pl.ds(n * 16, 16)
+        for i in range(2):
+            copies.append(
+                pltpu.make_async_copy(refs[i].at[rows], refs[4 + i].at[rows], sem.at[4 + 2 * n + i])
+            )
     for copy in copies:
         copy.start()
     for copy in copies:
@@ -619,7 +625,7 @@
         out_shape=tuple(jax.ShapeDtypeStruct(shape, kind) for shape, kind in shapes),
         in_specs=[anyw] * 4,
         out_specs=(anyw,) * 4,
-        scratch_shapes=[pltpu.SemaphoreType.DMA((4,))],
+        scratch_shapes=[pltpu.SemaphoreType.DMA((12,))],
         compiler_params=pltpu.CompilerParams(vmem_limit_bytes=1 << 20),
     )(*[pltpu.with_memory_space_constraint(a, pltpu.VMEM) for a in results])
     return out.reshape(1, CD, cells), fgrad.reshape(1, CD, cells), wgrad, ggrad.T

time: 93.2 us -> 94.8 us (1.017)
  Pallas kernels: 92.3 us -> 93.8 us
    pallas_call x1, Pallas kernels: 89.6 us -> 91.1 us  [body(): pl.pallas_call(kernel, out_shape=tuple((pltpu.VMEM(shape, kind) for shape...]
where the time goes in v2:
time: 94.8 us; the launch traced here: 94.6 us
  Pallas kernels  93.8 us (99%)
    pallas_call x1, Pallas kernels, body(): pl.pallas_call(kernel, out_shape=tuple((pltpu.VMEM(shape, kind) for shape...  91.1 us
    pallas_call x1, Pallas kernels, body(): pl.pallas_call(finish, out_shape=tuple((jax.ShapeDtypeStruct(shape, kind)...  2.74 us

profile of v2, /device:TPU:1, one launch (start us, length us, event | category | flops | bytes accessed | tf_op | source)
XLA Modules:
  0.0 94.6 jit_solution(9466832120363849)
XLA Ops:
  0.6 91.1 %shard_map.84 = (bf16[64,23040]{1,0:T(8,128)(2,1)S(1)}, bf16[64,23040]{1,0:T(8,128)(2,1)S(1)}, f32[2,64,256]{2,1,0:T(8,128)S(1)}, f32[64,640]{1,0:T(8,128)S(1)}) custom-call(bf16[64,23040]{1,0:T(8,128)(2,1)} %bitcast.7, bf16[2,64,256]{2,1,0:T(8,128)(2,1)} %w_ref.1, bf16[64,640]{1,0:T(8,128)(2,1)} %bitcast.9, bf16[64,23040]{1,0:T(8,128)(2,1)} %bitcast.8, ...), custom_call_target="tpu_custom_call" | custom-call | tf_op jit(solution)/shard_map/pallas_call | solution.py:574
  91.7 2.7 %shard_map.85 = (bf16[64,23040]{1,0:T(8,128)(2,1)}, bf16[64,23040]{1,0:T(8,128)(2,1)}, f32[2,64,256]{2,1,0:T(8,128)}, f32[64,640]{1,0:T(8,128)}) custom-call(bf16[64,23040]{1,0:T(8,128)(2,1)S(1)} %get-tuple-element.12.refs_0_, bf16[64,23040]{1,0:T(8,128)(2,1)S(1)} %get-tuple-element.13.refs_1_, f32[2,64,256]{2,1,0:T(8,128)S(1)} %get-tuple-element.14.refs_2_, ...), custom_call_target="tpu_custom_call" | custom-call | tf_op jit(solution)/shard_map/pallas_call | solution.py:623
